TPU v7x, 768 devices: a whole 4x8x12 slice. The times are simulated.
768 devices in a mesh: lat: 96 (over z_lo, y, x), lon: 8 (over z_hi, core).
Axes of the slice: x: 4, y: 8, z: 12 (z_hi: 4, z_lo: 3; z = z_hi * 3 + z_lo), core: 2. Of those that a mesh axis runs over, the one named last changes fastest.
Arguments:
- grad_output: bfloat16 [768, 1440, 128], P('lat', 'lon'), may hold values from -6 to 6
- band_rows: int32 [96], replicated, may hold values from 1 to 8, 721 in all
- legendre: float32 [192, 360, 768], P('lat'), may hold values from -0.21875 to 0.21875
- quad_weights: float32 [768], replicated, may hold values from 0.3 to 3
- spectral_filter: float32 [2, 360, 128], replicated, may hold values from -6 to 6
- disco_kernel: float32 [768, 9, 9], replicated, may hold values from -2 to 2
- disco_weight: bfloat16 [128, 9, 128], replicated, may hold values from -0.1875 to 0.1875
Outputs:
- grad_input: bfloat16 [768, 1440, 128], P('lat', 'lon')
Inputs may be any that keep to these rules, and one draw needn't show every extreme that they name: Bands follow each other from north to south; the live rows of band b fill its first band_rows[b] slots, and all bands together hold 721 rows.
All inputs are finite; a program needn't handle non-finite values.
Results may differ from a plain program's by a relative error of at most 0.0048.
Values may be sent and summed in bfloat16 or wider, within the bound.
A program may use at most 64 MiB of HBM per device.

v0:
```python
import jax
import jax.numpy as jnp
import ml_dtypes
import numpy as np
from jax import lax
from jax.experimental import pallas as pl
from jax.experimental.pallas import tpu as pltpu
from jax.sharding import PartitionSpec as P

MESH = pl.DeviceIdType.MESH
BF16 = jnp.bfloat16
F32 = jnp.float32

ROWS = 8
LON = 180
LONP = 192
CH = 128
LON_DEV = 8
LAT_DEV = 96
SHARE = CH // LON_DEV
MODES = 192
COEF = 2 * MODES
DEG = 360
DEGP = 384
SLOTS = LAT_DEV * ROWS
TAPS = 9
KINDS = 9
EDGE = 8


def trig_tables():
    points = LON * LON_DEV
    position = np.arange(points)[:, None]
    wavenumber = np.arange(MODES)[None, :]
    angle = (wavenumber * position % points) * (2.0 * np.pi / points)
    table = np.stack([np.cos(angle), -np.sin(angle)], axis=2) * points**-0.5
    blocks = np.zeros((LON_DEV, LONP, COEF))
    blocks[:, :LON] = table.reshape(LON_DEV, LON, COEF)
    inverse = blocks.astype(ml_dtypes.bfloat16)
    forward = np.ascontiguousarray(inverse.reshape(LON_DEV * LONP, COEF).T)
    return forward, inverse


def exchange_groups(rows, group_bit):
    rows = list(rows)
    for half in (4, 2, 1):
        low = (group_bit & half) == 0
        for r in range(ROWS):
            if r & half:
                continue
            a, b = rows[r], rows[r + half]
            rows[r] = jnp.where(low, a, pltpu.roll(b, SHARE * half, 1))
            rows[r + half] = jnp.where(low, pltpu.roll(a, CH - SHARE * half, 1), b)
    return rows


def kernel(
    rows_ref, g_ref, leg_ref, qw_ref, filt_ref, kern_ref, w_ref, tf_ref, ti_ref, out_ref,
    gv, xf, ext, send1, recv1, lat_s1, lat_r1, lat_s2, lat_r2, send2, recv2,
    row_s, row_r, cell_s, cell_r,
    legv, legb, legt, qwv, filtv, filtr, kernv, kpad, kbc, wv, wf, weff,
    tfv, tiv, dsum, coltmp, rhs, zed, pick, outf,
    load_sem, own_sem, s1, r1, s2, r2, hs, hr, ls, lr,
):
    a = lax.axis_index("lat")
    d = lax.axis_index("lon")
    up, down = lax.rem(a + LAT_DEV - 1, LAT_DEV), lax.rem(a + 1, LAT_DEV)
    west, east = lax.rem(d + LON_DEV - 1, LON_DEV), lax.rem(d + 1, LON_DEV)

    def load(i, src, dst):
        copy = pltpu.make_async_copy(src, dst, load_sem.at[i])
        copy.start()
        return copy

    load_g = load(0, g_ref, gv)
    load_leg = load(1, leg_ref, legv)
    load_qw = load(2, qw_ref, qwv)
    load_filt = load(3, filt_ref, filtv)
    load_kern = load(4, kern_ref, kernv)
    load_w = load(5, w_ref, wv)
    load_tf = load(6, tf_ref, tfv)
    load_ti = load(7, ti_ref, tiv)

    barrier = pltpu.get_barrier_semaphore()

    def greet(k, carry):
        pl.semaphore_signal(
            barrier, inc=1, device_id=(lax.rem(a + k, LAT_DEV), d), device_id_type=MESH
        )
        return carry

    lax.fori_loop(1, LAT_DEV, greet, 0)
    for k in range(1, LON_DEV):
        pl.semaphore_signal(
            barrier, inc=1, device_id=(a, lax.rem(d + k, LON_DEV)), device_id_type=MESH
        )
    for lat in (up, down):
        for lon in (west, east):
            pl.semaphore_signal(barrier, inc=1, device_id=(lat, lon), device_id_type=MESH)

    live = rows_ref[a]
    load_g.wait()
    slot3 = lax.broadcasted_iota(jnp.int32, (LON, ROWS, CH), 1)
    masked = jnp.where(slot3 < live, gv[...].astype(F32), 0.0)
    xf[pl.ds(0, LON * ROWS), :] = masked.reshape(LON * ROWS, CH)
    xf[pl.ds(LON * ROWS, (LONP - LON) * ROWS), :] = jnp.zeros(((LONP - LON) * ROWS, CH), F32)
    group16 = lax.broadcasted_iota(jnp.int32, (16, CH), 1) // SHARE

    def spread(chunk, carry):
        first = pl.multiple_of(chunk * 16, 16)
        rows = [xf[pl.ds(first * ROWS + r, 16, stride=ROWS), :] for r in range(ROWS)]
        last_row = jnp.zeros((16, CH), F32)
        for r in range(ROWS):
            ext[r + 1, pl.ds(first + EDGE, 16), :] = rows[r]
            last_row = jnp.where(live == r + 1, rows[r], last_row)
        row_s[0, pl.ds(first, 16), :] = last_row.astype(BF16)
        row_s[1, pl.ds(first, 16), :] = rows[0].astype(BF16)
        swapped = exchange_groups(rows, group16)
        for p in range(LON_DEV):
            send1[p, pl.ds(first, 16), :] = swapped[p].astype(BF16)
        return carry

    lax.fori_loop(0, LONP // 16, spread, 0)

    pl.semaphore_wait(barrier, LAT_DEV - 1 + LON_DEV - 1 + 4)

    def partner(k):
        z, core = d // 2, lax.rem(d, 2)
        return lax.rem(z + k // 2, 4) * 2 + lax.rem(core + k % 2, 2)

    far_first = (4, 5, 2, 6, 3, 7, 1)

    def swap1(k):
        p = partner(k)
        return pltpu.make_async_remote_copy(
            src_ref=send1.at[p], dst_ref=recv1.at[d], send_sem=s1.at[k], recv_sem=r1.at[k],
            device_id=(a, p), device_id_type=MESH,
        )

    for k in far_first:
        swap1(k).start()
    own1 = pltpu.make_async_copy(send1.at[d], recv1.at[d], own_sem.at[0])
    own1.start()

    first_col = xf[pl.ds(0, ROWS), :]
    last_col = xf[pl.ds((LON - 1) * ROWS, ROWS), :]
    slot8 = lax.broadcasted_iota(jnp.int32, (ROWS, CH), 0)
    pad8 = jnp.zeros((ROWS, CH), F32)

    def cell_of(column, slot):
        cell = jnp.sum(jnp.where(slot8 == slot, column, 0.0), axis=0, keepdims=True)
        return jnp.broadcast_to(cell, (16, CH))

    cell_s[0] = jnp.concatenate([last_col, pad8], axis=0).astype(BF16)
    cell_s[1] = jnp.concatenate([first_col, pad8], axis=0).astype(BF16)
    cell_s[2] = cell_of(last_col, live - 1).astype(BF16)
    cell_s[3] = cell_of(first_col, live - 1).astype(BF16)
    cell_s[4] = cell_of(last_col, 0).astype(BF16)
    cell_s[5] = cell_of(first_col, 0).astype(BF16)
    targets = ((a, east), (a, west), (down, east), (down, west), (up, east), (up, west))
    edges = [
        pltpu.make_async_remote_copy(
            src_ref=cell_s.at[i], dst_ref=cell_r.at[i], send_sem=hs.at[i], recv_sem=hr.at[i],
            device_id=target, device_id_type=MESH,
        )
        for i, target in enumerate(targets)
    ] + [
        pltpu.make_async_remote_copy(
            src_ref=row_s.at[i], dst_ref=row_r.at[i], send_sem=hs.at[6 + i], recv_sem=hr.at[6 + i],
            device_id=(lat, d), device_id_type=MESH,
        )
        for i, lat in enumerate((down, up))
    ]
    for copy in edges:
        copy.start()

    load_leg.wait()
    load_qw.wait()
    legb[...] = jnp.zeros_like(legb)
    for mm in range(2):
        legb[mm, pl.ds(0, DEG), :] = legv[mm].astype(BF16)
    zero_rows = jnp.zeros((DEGP - DEG, CH), F32)

    for mm in range(2):
        for block in range(SLOTS // CH):
            at = block * CH
            tile = legv[mm, :, pl.ds(at, CH)] * qwv[:, pl.ds(at, CH)]
            tile = jnp.concatenate([tile, zero_rows], axis=0)
            legt[mm, pl.ds(at, CH), :] = tile.T.astype(BF16)

    load_filt.wait()
    lane = lax.broadcasted_iota(jnp.int32, (DEG, CH), 1)
    filtr[...] = jnp.zeros_like(filtr)
    for part in range(2):
        mine = pltpu.roll(filtv[part], lax.rem(CH - SHARE * d, CH), 1)
        mine = jnp.where(lane < SHARE, mine, 0.0)
        for step in (SHARE, 2 * SHARE, 4 * SHARE):
            mine = mine + pltpu.roll(mine, step, 1)
        filtr[part, pl.ds(0, DEG), :] = mine

    band_row = lax.broadcasted_iota(jnp.int32, (LAT_DEV, SLOTS), 0)
    band_col = lax.broadcasted_iota(jnp.int32, (LAT_DEV, SLOTS), 1) // ROWS
    pick[...] = jnp.where(band_row == band_col, 1.0, 0.0).astype(BF16)

    load_kern.wait()
    kpad[...] = jnp.zeros_like(kpad)
    for t in range(TAPS):
        kpad[pl.ds(16 * t, KINDS), :] = kernv[t]
    above_slot = up * ROWS + rows_ref[up] - 1
    here = lax.broadcasted_iota(jnp.int32, (SLOTS, CH), 1)
    slot_row = lax.broadcasted_iota(jnp.int32, (SLOTS, CH), 0)
    source = jnp.where(here - 1 < live, a * ROWS + here - 1, down * ROWS)
    source = jnp.where(here == 0, above_slot, source)
    one_hot = jnp.where(slot_row == source, 1.0, 0.0)
    chosen = jnp.dot(kpad[...], one_hot, precision=lax.Precision.HIGHEST, preferred_element_type=F32)
    for row in range(ROWS + 2):
        kbc[row] = jnp.broadcast_to(chosen[:, row : row + 1], (16 * TAPS, CH))

    load_w.wait()
    wf[...] = wv[...].astype(F32)

    def weights(step, carry):
        row, half = step // 2, lax.rem(step, 2)
        o = pl.multiple_of(half * 64, 64)
        for t in range(TAPS):
            total = None
            for k in range(KINDS):
                part = wf[k, pl.ds(o, 64), :] * kbc[row, pl.ds(16 * t + k, 1), :]
                total = part if total is None else total + part
            tap_row, tap_col = t // 3, t % 3
            weff[row, pl.ds(tap_col * CH + o, 64), pl.ds(tap_row * CH, CH)] = total.astype(BF16)
        return carry

    lax.fori_loop(0, 2 * (ROWS + 2), weights, 0)

    for copy in edges:
        copy.wait()
    has_above = a > 0
    has_below = a < LAT_DEV - 1
    above_row = jnp.where(has_above, row_r[0].astype(F32), 0.0)
    below_row = jnp.where(has_below, row_r[1].astype(F32), 0.0)
    ext[0, pl.ds(EDGE, LONP), :] = above_row
    for slot in range(1, ROWS):
        old = ext[slot + 1, pl.ds(EDGE, LONP), :]
        ext[slot + 1, pl.ds(EDGE, LONP), :] = jnp.where(live == slot, below_row, old)
    ext[ROWS + 1, pl.ds(EDGE, LONP), :] = jnp.where(live == ROWS, below_row, 0.0)
    for side, at in ((0, EDGE - 1), (1, EDGE + LON)):
        slots = cell_r[side].astype(F32)
        above_cell = jnp.where(has_above, cell_r[2 + side].astype(F32), 0.0)
        below_cell = jnp.where(has_below, cell_r[4 + side].astype(F32), 0.0)
        ext[0, pl.ds(at, 1), :] = above_cell[0:1]
        for slot in range(ROWS + 1):
            edge_cell = jnp.where(live == slot, below_cell[0:1], slots[slot : slot + 1])
            ext[slot + 1, pl.ds(at, 1), :] = edge_cell

    dsum[...] = jnp.zeros_like(dsum)
    for slot in range(ROWS):
        dsum[slot + 2] = xf[pl.ds(slot, LONP, stride=ROWS), :]

    def stencil(row, carry):
        field = jnp.concatenate(
            [ext[row, pl.ds(EDGE - b, LONP), :] for b in (-1, 0, 1)], axis=1
        ).astype(BF16)
        taps = jnp.dot(field, weff[row], preferred_element_type=F32)
        for step in (-1, 0, 1):
            index = (step + 1) * CH
            dsum[row + step + 1] += taps[:, index : index + CH]
        return carry

    lax.fori_loop(0, ROWS + 2, stencil, 0)

    own1.wait()
    for k in far_first:
        swap1(k).wait()
    load_tf.wait()
    spectra = jnp.dot(
        tfv[...], recv1[...].reshape(LON_DEV * LONP, CH), preferred_element_type=F32
    )
    lat_s1[...] = spectra.astype(BF16).reshape(LAT_DEV, 4, CH)

    def all_lat(sent, got, which):
        own = pltpu.make_async_copy(sent.at[a], got.at[a], lr.at[which])
        own.start()

        def send(k, carry):
            j = lax.rem(a + k, LAT_DEV)
            pltpu.make_async_remote_copy(
                src_ref=sent.at[j], dst_ref=got.at[a], send_sem=ls.at[which],
                recv_sem=lr.at[which], device_id=(j, d), device_id_type=MESH,
            ).start()
            return carry

        lax.fori_loop(1, LAT_DEV, send, 0)
        pltpu.make_async_copy(sent, got, lr.at[which]).wait()

    all_lat(lat_s1, lat_r1, 0)

    coltmp[...] = lat_r1[...].astype(F32).reshape(COEF, CH)
    block_slot = lax.broadcasted_iota(jnp.int32, (LAT_DEV, ROWS, CH), 1)
    block_group = lax.broadcasted_iota(jnp.int32, (LAT_DEV, ROWS, CH), 2) // SHARE
    diagonal = block_slot == block_group
    for q in range(4):
        column = coltmp[pl.ds(q, LAT_DEV, stride=4), :]
        wide = jnp.where(diagonal, column[:, None, :], 0.0)
        rhs[:, pl.ds(q * CH, CH)] = wide.reshape(SLOTS, CH).astype(BF16)
    for mm in range(2):
        coef = jnp.dot(legb[mm], rhs[:, pl.ds(mm * 2 * CH, 2 * CH)], preferred_element_type=F32)
        parts = []
        for part in range(2):
            folded = coef[:, part * CH : (part + 1) * CH]
            for step in (SHARE, 2 * SHARE, 4 * SHARE):
                folded = folded + pltpu.roll(folded, step, 1)
            parts.append(folded)
        real, imag = parts
        fr, fi = filtr[0], filtr[1]
        filtered = jnp.concatenate([fr * real + fi * imag, fr * imag - fi * real], axis=1)
        back = jnp.dot(legt[mm], filtered.astype(BF16), preferred_element_type=F32)
        for part in range(2):
            wide = back[:, part * CH : (part + 1) * CH].reshape(LAT_DEV, ROWS, CH)
            wide = jnp.where(diagonal, wide, 0.0).astype(BF16)
            zed[:, pl.ds((2 * mm + part) * CH, CH)] = wide.reshape(SLOTS, CH)
    returned = jnp.dot(pick[...], zed[...], preferred_element_type=F32)
    for q in range(4):
        coltmp[pl.ds(q, LAT_DEV, stride=4), :] = returned[:, q * CH : (q + 1) * CH]
    lat_s2[...] = coltmp[...].astype(BF16).reshape(LAT_DEV, 4, CH)
    all_lat(lat_s2, lat_r2, 1)

    load_ti.wait()
    modes = lat_r2[...].reshape(COEF, CH)

    def block_of(p):
        send2[p] = jnp.dot(tiv[p], modes, preferred_element_type=F32).astype(BF16)

    def swap2(k):
        p = partner(k)
        return pltpu.make_async_remote_copy(
            src_ref=send2.at[p], dst_ref=recv2.at[d], send_sem=s2.at[k], recv_sem=r2.at[k],
            device_id=(a, p), device_id_type=MESH,
        )

    for k in far_first:
        block_of(partner(k))
        swap2(k).start()
    block_of(d)
    own2 = pltpu.make_async_copy(send2.at[d], recv2.at[d], own_sem.at[1])
    own2.start()
    own2.wait()
    for k in far_first:
        swap2(k).wait()

    def gather(chunk, carry):
        first = pl.multiple_of(chunk * 16, 16)
        blocks = [recv2[e, pl.ds(first, 16), :].astype(F32) for e in range(LON_DEV)]
        rows = exchange_groups(blocks, group16)
        for r in range(ROWS):
            total = dsum[r + 2, pl.ds(first, 16), :] + rows[r]
            outf[pl.ds(first * ROWS + r, 16, stride=ROWS), :] = jnp.where(r < live, total, 0.0)
        return carry

    lax.fori_loop(0, LONP // 16, gather, 0)
    out_ref[...] = outf[pl.ds(0, LON * ROWS), :].astype(BF16).reshape(LON, ROWS, CH)

    for which, sent in ((0, lat_s1), (1, lat_s2)):
        most = sent.at[pl.ds(0, LAT_DEV - 1)]
        pltpu.make_async_copy(most, most, ls.at[which]).wait()


def on_device(grad_output, band_rows, legendre, quad_weights, spectral_filter, disco_kernel, disco_weight):
    forward, inverse = trig_tables()
    any_space = pl.BlockSpec(memory_space=pl.ANY)
    vmem = pltpu.VMEM
    dma = pltpu.SemaphoreType.DMA
    out = pl.pallas_call(
        kernel,
        out_shape=jax.ShapeDtypeStruct((LON, ROWS, CH), BF16),
        in_specs=[pl.BlockSpec(memory_space=pltpu.SMEM)] + [any_space] * 8,
        out_specs=pl.BlockSpec(memory_space=pltpu.VMEM),
        scratch_shapes=[
            vmem((LON, ROWS, CH), BF16),
            vmem((LONP * ROWS, CH), F32),
            vmem((ROWS + 2, LONP + 2 * EDGE, CH), F32),
            vmem((LON_DEV, LONP, CH), BF16),
            vmem((LON_DEV, LONP, CH), BF16),
            vmem((LAT_DEV, 4, CH), BF16),
            vmem((LAT_DEV, 4, CH), BF16),
            vmem((LAT_DEV, 4, CH), BF16),
            vmem((LAT_DEV, 4, CH), BF16),
            vmem((LON_DEV, LONP, CH), BF16),
            vmem((LON_DEV, LONP, CH), BF16),
            vmem((2, LONP, CH), BF16),
            vmem((2, LONP, CH), BF16),
            vmem((6, 16, CH), BF16),
            vmem((6, 16, CH), BF16),
            vmem((2, DEG, SLOTS), F32),
            vmem((2, DEGP, SLOTS), BF16),
            vmem((2, SLOTS, DEGP), BF16),
            vmem((1, SLOTS), F32),
            vmem((2, DEG, CH), F32),
            vmem((2, DEGP, CH), F32),
            vmem((TAPS, KINDS, SLOTS), F32),
            vmem((16 * TAPS, SLOTS), F32),
            vmem((ROWS + 2, 16 * TAPS, CH), F32),
            vmem((KINDS, CH, CH), BF16),
            vmem((KINDS, CH, CH), F32),
            vmem((ROWS + 2, 3 * CH, 3 * CH), BF16),
            vmem((COEF, LON_DEV * LONP), BF16),
            vmem((LON_DEV, LONP, COEF), BF16),
            vmem((ROWS + 4, LONP, CH), F32),
            vmem((COEF, CH), F32),
            vmem((SLOTS, 4 * CH), BF16),
            vmem((SLOTS, 4 * CH), BF16),
            vmem((LAT_DEV, SLOTS), BF16),
            vmem((LONP * ROWS, CH), F32),
            dma((8,)),
            dma((2,)),
            dma((8,)),
            dma((8,)),
            dma((8,)),
            dma((8,)),
            dma((8,)),
            dma((8,)),
            dma((2,)),
            dma((2,)),
        ],
        compiler_params=pltpu.CompilerParams(
            collective_id=0, has_side_effects=True, vmem_limit_bytes=56 * 2**20
        ),
    )(
        band_rows,
        jnp.transpose(grad_output, (1, 0, 2)),
        legendre,
        quad_weights.reshape(1, SLOTS),
        spectral_filter,
        jnp.transpose(disco_kernel, (1, 2, 0)),
        jnp.transpose(disco_weight, (1, 0, 2)),
        jnp.asarray(forward),
        jnp.asarray(inverse),
    )
    return jnp.transpose(out, (1, 0, 2))


def solution(mesh):
    placed = (P("lat", "lon", None), P(), P("lat", None, None), P(), P(), P(), P())
    return jax.shard_map(
        on_device, mesh=mesh, in_specs=placed, out_specs=P("lat", "lon", None), check_vma=False
    )
```

profile of v0, /device:TPU:1, one launch (start us, length us, event | category | flops | bytes accessed | tf_op | source)
XLA Modules:
  0.0 83.3 jit_solution(1391924796275785928)
XLA Ops:
  0.0 1.3 %reshape.3.qw_ref = f32[1,768]{1,0:T(1,128)} reshape(f32[768]{0:T(1024)} %param.12) | data formatting | bytes 6144 | tf_op jit(solution)/shard_map/reshape | solution.py:432
  1.3 80.2 %shard_map.91 = bf16[180,8,128]{2,1,0:T(8,128)(2,1)} custom-call(s32[96]{0:T(128)} %rows_ref.1, bf16[180,8,128]{2,1,0:T(8,128)(2,1)} %bitcast.6, f32[2,360,768]{2,1,0:T(8,128)} %leg_ref.1, f32[1,768]{1,0:T(1,128)} %reshape.3.qw_ref, f32[2,360,128]{2,1,0:T(8,128)} %filt_ref.1, f32[9,9,768]{2,1,0:T(8,128)} %bitcast.5, bf16[9,128,128]{2,1,0:T(8,128)(2,1)} %bitcast.7, ...), custom_call_target="tpu_custom_call" | custom-call | tf_op jit(solution)/shard_map/pallas_call | solution.py:373
  81.5 1.7 %copy.11 = bf16[8,180,128]{2,0,1:T(8,128)(2,1)} copy(bf16[8,180,128]{2,0,1:T(8,128)(2,1)} %bitcast.4) | data formatting | bytes 737280
where the time goes:
time: 83.5 us; the launch traced here: 83.3 us
  Pallas kernels  80.2 us (96%)
  local copies, waits for them, and re-layouts  3.02 us (4%)
    pallas_call x1, Pallas kernels, on_device(): pl.pallas_call(kernel, out_shape=jax.ShapeDtypeStruct((LON, ROWS, CH), BF...  80.2 us
    unnamed x1, local copies, waits for them, and re-layouts  1.75 us

commit v1 on v0

--- a/solution.py
+++ b/solution.py
@@ -55,10 +55,10 @@
 
 
 def kernel(
-    rows_ref, g_ref, leg_ref, qw_ref, filt_ref, kern_ref, w_ref, tf_ref, ti_ref, out_ref,
+    rows_ref, qw_ref, g_ref, leg_ref, filt_ref, kern_ref, w_ref, tf_ref, ti_ref, out_ref,
     gv, xf, ext, send1, recv1, lat_s1, lat_r1, lat_s2, lat_r2, send2, recv2,
     row_s, row_r, cell_s, cell_r,
-    legv, legb, legt, qwv, filtv, filtr, kernv, kpad, kbc, wv, wf, weff,
+    legv, legb, legt, filtv, filtr, kernv, kpad, kbc, wv, wf, weff,
     tfv, tiv, dsum, coltmp, rhs, zed, pick, outf,
     load_sem, own_sem, s1, r1, s2, r2, hs, hr, ls, lr,
 ):
@@ -73,23 +73,18 @@
         return copy
 
     load_g = load(0, g_ref, gv)
-    load_leg = load(1, leg_ref, legv)
-    load_qw = load(2, qw_ref, qwv)
-    load_filt = load(3, filt_ref, filtv)
-    load_kern = load(4, kern_ref, kernv)
-    load_w = load(5, w_ref, wv)
-    load_tf = load(6, tf_ref, tfv)
-    load_ti = load(7, ti_ref, tiv)
 
     barrier = pltpu.get_barrier_semaphore()
 
+    def lat_after(k):
+        j = a + k
+        return jnp.where(j >= LAT_DEV, j - LAT_DEV, j)
+
     def greet(k, carry):
-        pl.semaphore_signal(
-            barrier, inc=1, device_id=(lax.rem(a + k, LAT_DEV), d), device_id_type=MESH
-        )
+        pl.semaphore_signal(barrier, inc=1, device_id=(lat_after(k), d), device_id_type=MESH)
         return carry
 
-    lax.fori_loop(1, LAT_DEV, greet, 0)
+    lax.fori_loop(1, LAT_DEV, greet, 0, unroll=5)
     for k in range(1, LON_DEV):
         pl.semaphore_signal(
             barrier, inc=1, device_id=(a, lax.rem(d + k, LON_DEV)), device_id_type=MESH
@@ -97,6 +92,12 @@
     for lat in (up, down):
         for lon in (west, east):
             pl.semaphore_signal(barrier, inc=1, device_id=(lat, lon), device_id_type=MESH)
+    load_leg = load(1, leg_ref, legv)
+    load_filt = load(2, filt_ref, filtv)
+    load_kern = load(3, kern_ref, kernv)
+    load_w = load(4, w_ref, wv)
+    load_tf = load(5, tf_ref, tfv)
+    load_ti = load(6, ti_ref, tiv)
 
     live = rows_ref[a]
     load_g.wait()
@@ -106,21 +107,12 @@
     xf[pl.ds(LON * ROWS, (LONP - LON) * ROWS), :] = jnp.zeros(((LONP - LON) * ROWS, CH), F32)
     group16 = lax.broadcasted_iota(jnp.int32, (16, CH), 1) // SHARE
 
-    def spread(chunk, carry):
-        first = pl.multiple_of(chunk * 16, 16)
+    for chunk in range(LONP // 16):
+        first = chunk * 16
         rows = [xf[pl.ds(first * ROWS + r, 16, stride=ROWS), :] for r in range(ROWS)]
-        last_row = jnp.zeros((16, CH), F32)
-        for r in range(ROWS):
-            ext[r + 1, pl.ds(first + EDGE, 16), :] = rows[r]
-            last_row = jnp.where(live == r + 1, rows[r], last_row)
-        row_s[0, pl.ds(first, 16), :] = last_row.astype(BF16)
-        row_s[1, pl.ds(first, 16), :] = rows[0].astype(BF16)
         swapped = exchange_groups(rows, group16)
         for p in range(LON_DEV):
             send1[p, pl.ds(first, 16), :] = swapped[p].astype(BF16)
-        return carry
-
-    lax.fori_loop(0, LONP // 16, spread, 0)
 
     pl.semaphore_wait(barrier, LAT_DEV - 1 + LON_DEV - 1 + 4)
 
@@ -142,6 +134,16 @@
     own1 = pltpu.make_async_copy(send1.at[d], recv1.at[d], own_sem.at[0])
     own1.start()
 
+    for r in range(ROWS):
+        row = xf[pl.ds(r, LONP, stride=ROWS), :]
+        ext[r + 1, pl.ds(EDGE, LONP), :] = row
+        dsum[r + 2] = row
+        if r == 0:
+            row_s[1] = row.astype(BF16)
+            last_row = row
+        else:
+            last_row = jnp.where(live == r + 1, row, last_row)
+    row_s[0] = last_row.astype(BF16)
     first_col = xf[pl.ds(0, ROWS), :]
     last_col = xf[pl.ds((LON - 1) * ROWS, ROWS), :]
     slot8 = lax.broadcasted_iota(jnp.int32, (ROWS, CH), 0)
@@ -175,7 +177,6 @@
         copy.start()
 
     load_leg.wait()
-    load_qw.wait()
     legb[...] = jnp.zeros_like(legb)
     for mm in range(2):
         legb[mm, pl.ds(0, DEG), :] = legv[mm].astype(BF16)
@@ -184,8 +185,7 @@
     for mm in range(2):
         for block in range(SLOTS // CH):
             at = block * CH
-            tile = legv[mm, :, pl.ds(at, CH)] * qwv[:, pl.ds(at, CH)]
-            tile = jnp.concatenate([tile, zero_rows], axis=0)
+            tile = jnp.concatenate([legv[mm, :, pl.ds(at, CH)], zero_rows], axis=0)
             legt[mm, pl.ds(at, CH), :] = tile.T.astype(BF16)
 
     load_filt.wait()
@@ -233,42 +233,6 @@
 
     lax.fori_loop(0, 2 * (ROWS + 2), weights, 0)
 
-    for copy in edges:
-        copy.wait()
-    has_above = a > 0
-    has_below = a < LAT_DEV - 1
-    above_row = jnp.where(has_above, row_r[0].astype(F32), 0.0)
-    below_row = jnp.where(has_below, row_r[1].astype(F32), 0.0)
-    ext[0, pl.ds(EDGE, LONP), :] = above_row
-    for slot in range(1, ROWS):
-        old = ext[slot + 1, pl.ds(EDGE, LONP), :]
-        ext[slot + 1, pl.ds(EDGE, LONP), :] = jnp.where(live == slot, below_row, old)
-    ext[ROWS + 1, pl.ds(EDGE, LONP), :] = jnp.where(live == ROWS, below_row, 0.0)
-    for side, at in ((0, EDGE - 1), (1, EDGE + LON)):
-        slots = cell_r[side].astype(F32)
-        above_cell = jnp.where(has_above, cell_r[2 + side].astype(F32), 0.0)
-        below_cell = jnp.where(has_below, cell_r[4 + side].astype(F32), 0.0)
-        ext[0, pl.ds(at, 1), :] = above_cell[0:1]
-        for slot in range(ROWS + 1):
-            edge_cell = jnp.where(live == slot, below_cell[0:1], slots[slot : slot + 1])
-            ext[slot + 1, pl.ds(at, 1), :] = edge_cell
-
-    dsum[...] = jnp.zeros_like(dsum)
-    for slot in range(ROWS):
-        dsum[slot + 2] = xf[pl.ds(slot, LONP, stride=ROWS), :]
-
-    def stencil(row, carry):
-        field = jnp.concatenate(
-            [ext[row, pl.ds(EDGE - b, LONP), :] for b in (-1, 0, 1)], axis=1
-        ).astype(BF16)
-        taps = jnp.dot(field, weff[row], preferred_element_type=F32)
-        for step in (-1, 0, 1):
-            index = (step + 1) * CH
-            dsum[row + step + 1] += taps[:, index : index + CH]
-        return carry
-
-    lax.fori_loop(0, ROWS + 2, stencil, 0)
-
     own1.wait()
     for k in far_first:
         swap1(k).wait()
@@ -283,14 +247,14 @@
         own.start()
 
         def send(k, carry):
-            j = lax.rem(a + k, LAT_DEV)
+            j = lat_after(k)
             pltpu.make_async_remote_copy(
                 src_ref=sent.at[j], dst_ref=got.at[a], send_sem=ls.at[which],
                 recv_sem=lr.at[which], device_id=(j, d), device_id_type=MESH,
             ).start()
             return carry
 
-        lax.fori_loop(1, LAT_DEV, send, 0)
+        lax.fori_loop(1, LAT_DEV, send, 0, unroll=5)
         pltpu.make_async_copy(sent, got, lr.at[which]).wait()
 
     all_lat(lat_s1, lat_r1, 0)
@@ -344,20 +308,54 @@
     block_of(d)
     own2 = pltpu.make_async_copy(send2.at[d], recv2.at[d], own_sem.at[1])
     own2.start()
+
+    for copy in edges:
+        copy.wait()
+    has_above = a > 0
+    has_below = a < LAT_DEV - 1
+    above_row = jnp.where(has_above, row_r[0].astype(F32), 0.0)
+    below_row = jnp.where(has_below, row_r[1].astype(F32), 0.0)
+    ext[0, pl.ds(EDGE, LONP), :] = above_row
+    for slot in range(1, ROWS):
+        old = ext[slot + 1, pl.ds(EDGE, LONP), :]
+        ext[slot + 1, pl.ds(EDGE, LONP), :] = jnp.where(live == slot, below_row, old)
+    ext[ROWS + 1, pl.ds(EDGE, LONP), :] = jnp.where(live == ROWS, below_row, 0.0)
+    for side, at in ((0, EDGE - 1), (1, EDGE + LON)):
+        slots = cell_r[side].astype(F32)
+        above_cell = jnp.where(has_above, cell_r[2 + side].astype(F32), 0.0)
+        below_cell = jnp.where(has_below, cell_r[4 + side].astype(F32), 0.0)
+        ext[0, pl.ds(at, 1), :] = above_cell[0:1]
+        for slot in range(ROWS + 1):
+            edge_cell = jnp.where(live == slot, below_cell[0:1], slots[slot : slot + 1])
+            ext[slot + 1, pl.ds(at, 1), :] = edge_cell
+
+    for spare in (0, 1, ROWS + 2, ROWS + 3):
+        dsum[spare] = jnp.zeros((LONP, CH), F32)
+
+    def stencil(row, carry):
+        field = jnp.concatenate(
+            [ext[row, pl.ds(EDGE - b, LONP), :] for b in (-1, 0, 1)], axis=1
+        ).astype(BF16)
+        taps = jnp.dot(field, weff[row], preferred_element_type=F32)
+        for step in (-1, 0, 1):
+            index = (step + 1) * CH
+            dsum[row + step + 1] += taps[:, index : index + CH]
+        return carry
+
+    lax.fori_loop(0, ROWS + 2, stencil, 0)
+
     own2.wait()
     for k in far_first:
         swap2(k).wait()
-
-    def gather(chunk, carry):
-        first = pl.multiple_of(chunk * 16, 16)
+    for chunk in range(LONP // 16):
+        first = chunk * 16
         blocks = [recv2[e, pl.ds(first, 16), :].astype(F32) for e in range(LON_DEV)]
         rows = exchange_groups(blocks, group16)
         for r in range(ROWS):
-            total = dsum[r + 2, pl.ds(first, 16), :] + rows[r]
-            outf[pl.ds(first * ROWS + r, 16, stride=ROWS), :] = jnp.where(r < live, total, 0.0)
-        return carry
-
-    lax.fori_loop(0, LONP // 16, gather, 0)
+            total = dsum[r + 2, pl.ds(first, 16), :]
+            total = total + rows[r] * qw_ref[a * ROWS + r]
+            total = jnp.where(r < live, total, 0.0)
+            outf[pl.ds(first * ROWS + r, 16, stride=ROWS), :] = total
     out_ref[...] = outf[pl.ds(0, LON * ROWS), :].astype(BF16).reshape(LON, ROWS, CH)
 
     for which, sent in ((0, lat_s1), (1, lat_s2)):
@@ -373,7 +371,7 @@
     out = pl.pallas_call(
         kernel,
         out_shape=jax.ShapeDtypeStruct((LON, ROWS, CH), BF16),
-        in_specs=[pl.BlockSpec(memory_space=pltpu.SMEM)] + [any_space] * 8,
+        in_specs=[pl.BlockSpec(memory_space=pltpu.SMEM)] * 2 + [any_space] * 7,
         out_specs=pl.BlockSpec(memory_space=pltpu.VMEM),
         scratch_shapes=[
             vmem((LON, ROWS, CH), BF16),
@@ -394,7 +392,6 @@
             vmem((2, DEG, SLOTS), F32),
             vmem((2, DEGP, SLOTS), BF16),
             vmem((2, SLOTS, DEGP), BF16),
-            vmem((1, SLOTS), F32),
             vmem((2, DEG, CH), F32),
             vmem((2, DEGP, CH), F32),
             vmem((TAPS, KINDS, SLOTS), F32),
@@ -427,9 +424,9 @@
         ),
     )(
         band_rows,
+        quad_weights,
         jnp.transpose(grad_output, (1, 0, 2)),
         legendre,
-        quad_weights.reshape(1, SLOTS),
         spectral_filter,
         jnp.transpose(disco_kernel, (1, 2, 0)),
         jnp.transpose(disco_weight, (1, 0, 2)),

time: 83.5 us -> 75.2 us (0.901)
  Pallas kernels: 80.2 us -> 73.2 us
  local copies, waits for them, and re-layouts: 3.02 us -> 1.75 us
    pallas_call x1, Pallas kernels: 80.2 us -> 73.2 us  [on_device(): pl.pallas_call(kernel, out_shape=jax.ShapeDtypeStruct((LON, ROWS, CH), BF...]
    reshape x1 -> x0, local copies, waits for them, and re-layouts: 1.27 us -> none  [on_device(): quad_weights.reshape(1, SLOTS)]
where the time goes in v1:
time: 75.2 us; the launch traced here: 75 us
  Pallas kernels  73.2 us (97%)
  local copies, waits for them, and re-layouts  1.75 us (2%)
    pallas_call x1, Pallas kernels, on_device(): pl.pallas_call(kernel, out_shape=jax.ShapeDtypeStruct((LON, ROWS, CH), BF...  73.2 us
    unnamed x1, local copies, waits for them, and re-layouts  1.75 us

profile of v1, /device:TPU:1, one launch (start us, length us, event | category | flops | bytes accessed | tf_op | source)
XLA Modules:
  0.0 75.0 jit_solution(16842723109785095885)
XLA Ops:
  0.0 73.2 %shard_map.91 = bf16[180,8,128]{2,1,0:T(8,128)(2,1)} custom-call(s32[96]{0:T(128)} %rows_ref.1, f32[768]{0:T(1024)} %qw_ref.1, bf16[180,8,128]{2,1,0:T(8,128)(2,1)} %bitcast.6, f32[2,360,768]{2,1,0:T(8,128)} %leg_ref.1, f32[2,360,128]{2,1,0:T(8,128)} %filt_ref.1, f32[9,9,768]{2,1,0:T(8,128)} %bitcast.5, bf16[9,128,128]{2,1,0:T(8,128)(2,1)} %bitcast.7, ...), custom_call_target="tpu_custom_call" | custom-call | tf_op jit(solution)/shard_map/pallas_call | solution.py:371
  73.2 1.7 %copy.11 = bf16[8,180,128]{2,0,1:T(8,128)(2,1)} copy(bf16[8,180,128]{2,0,1:T(8,128)(2,1)} %bitcast.4) | data formatting | bytes 737280

commit v2 on v1

--- a/solution.py
+++ b/solution.py
@@ -14,9 +14,11 @@
 ROWS = 8
 LON = 180
 LONP = 192
+HALF = LONP // 2
 CH = 128
 LON_DEV = 8
 LAT_DEV = 96
+X_DEV, Y_DEV, Z_DEV = 4, 8, 3
 SHARE = CH // LON_DEV
 MODES = 192
 COEF = 2 * MODES
@@ -72,7 +74,10 @@
         copy.start()
         return copy
 
-    load_g = load(0, g_ref, gv)
+    load_g = (
+        load(0, g_ref.at[pl.ds(0, HALF)], gv.at[pl.ds(0, HALF)]),
+        load(7, g_ref.at[pl.ds(HALF, LON - HALF)], gv.at[pl.ds(HALF, LON - HALF)]),
+    )
 
     barrier = pltpu.get_barrier_semaphore()
 
@@ -100,21 +105,7 @@
     load_ti = load(6, ti_ref, tiv)
 
     live = rows_ref[a]
-    load_g.wait()
-    slot3 = lax.broadcasted_iota(jnp.int32, (LON, ROWS, CH), 1)
-    masked = jnp.where(slot3 < live, gv[...].astype(F32), 0.0)
-    xf[pl.ds(0, LON * ROWS), :] = masked.reshape(LON * ROWS, CH)
-    xf[pl.ds(LON * ROWS, (LONP - LON) * ROWS), :] = jnp.zeros(((LONP - LON) * ROWS, CH), F32)
     group16 = lax.broadcasted_iota(jnp.int32, (16, CH), 1) // SHARE
-
-    for chunk in range(LONP // 16):
-        first = chunk * 16
-        rows = [xf[pl.ds(first * ROWS + r, 16, stride=ROWS), :] for r in range(ROWS)]
-        swapped = exchange_groups(rows, group16)
-        for p in range(LON_DEV):
-            send1[p, pl.ds(first, 16), :] = swapped[p].astype(BF16)
-
-    pl.semaphore_wait(barrier, LAT_DEV - 1 + LON_DEV - 1 + 4)
 
     def partner(k):
         z, core = d // 2, lax.rem(d, 2)
@@ -122,15 +113,32 @@
 
     far_first = (4, 5, 2, 6, 3, 7, 1)
 
-    def swap1(k):
+    def swap(sent, got, send_sem, recv_sem, half, k):
         p = partner(k)
+        part = pl.ds(half * HALF, HALF)
         return pltpu.make_async_remote_copy(
-            src_ref=send1.at[p], dst_ref=recv1.at[d], send_sem=s1.at[k], recv_sem=r1.at[k],
-            device_id=(a, p), device_id_type=MESH,
+            src_ref=sent.at[p, part], dst_ref=got.at[d, part], send_sem=send_sem.at[half, k],
+            recv_sem=recv_sem.at[half, k], device_id=(a, p), device_id_type=MESH,
         )
 
-    for k in far_first:
-        swap1(k).start()
+    for half in range(2):
+        load_g[half].wait()
+        count = HALF if half == 0 else LON - HALF
+        slot3 = lax.broadcasted_iota(jnp.int32, (count, ROWS, CH), 1)
+        masked = jnp.where(slot3 < live, gv[pl.ds(half * HALF, count)].astype(F32), 0.0)
+        xf[pl.ds(half * HALF * ROWS, count * ROWS), :] = masked.reshape(count * ROWS, CH)
+        if half == 1:
+            xf[pl.ds(LON * ROWS, (LONP - LON) * ROWS), :] = jnp.zeros(((LONP - LON) * ROWS, CH), F32)
+        for chunk in range(HALF // 16):
+            first = half * HALF + chunk * 16
+            rows = [xf[pl.ds(first * ROWS + r, 16, stride=ROWS), :] for r in range(ROWS)]
+            swapped = exchange_groups(rows, group16)
+            for p in range(LON_DEV):
+                send1[p, pl.ds(first, 16), :] = swapped[p].astype(BF16)
+        if half == 0:
+            pl.semaphore_wait(barrier, LAT_DEV - 1 + LON_DEV - 1 + 4)
+        for k in far_first:
+            swap(send1, recv1, s1, r1, half, k).start()
     own1 = pltpu.make_async_copy(send1.at[d], recv1.at[d], own_sem.at[0])
     own1.start()
 
@@ -216,45 +224,41 @@
     for row in range(ROWS + 2):
         kbc[row] = jnp.broadcast_to(chosen[:, row : row + 1], (16 * TAPS, CH))
 
-    load_w.wait()
-    wf[...] = wv[...].astype(F32)
-
-    def weights(step, carry):
-        row, half = step // 2, lax.rem(step, 2)
-        o = pl.multiple_of(half * 64, 64)
-        for t in range(TAPS):
-            total = None
-            for k in range(KINDS):
-                part = wf[k, pl.ds(o, 64), :] * kbc[row, pl.ds(16 * t + k, 1), :]
-                total = part if total is None else total + part
-            tap_row, tap_col = t // 3, t % 3
-            weff[row, pl.ds(tap_col * CH + o, 64), pl.ds(tap_row * CH, CH)] = total.astype(BF16)
-        return carry
-
-    lax.fori_loop(0, 2 * (ROWS + 2), weights, 0)
-
     own1.wait()
-    for k in far_first:
-        swap1(k).wait()
+    for half in range(2):
+        for k in far_first:
+            swap(send1, recv1, s1, r1, half, k).wait()
     load_tf.wait()
     spectra = jnp.dot(
         tfv[...], recv1[...].reshape(LON_DEV * LONP, CH), preferred_element_type=F32
     )
     lat_s1[...] = spectra.astype(BF16).reshape(LAT_DEV, 4, CH)
 
+    x_own, y_own, z_own = lax.rem(a, X_DEV), lax.rem(a // X_DEV, Y_DEV), a // (X_DEV * Y_DEV)
+    x_of = [lax.rem(x_own + dx, X_DEV) for dx in range(X_DEV)]
+    z_base = [lax.rem(z_own + dz, Z_DEV) * (X_DEV * Y_DEV) for dz in range(Z_DEV)]
+    across = [(dz, dx) for dz in (1, 2, 0) for dx in (2, 1, 3, 0)]
+
     def all_lat(sent, got, which):
         own = pltpu.make_async_copy(sent.at[a], got.at[a], lr.at[which])
         own.start()
 
-        def send(k, carry):
-            j = lat_after(k)
-            pltpu.make_async_remote_copy(
-                src_ref=sent.at[j], dst_ref=got.at[a], send_sem=ls.at[which],
-                recv_sem=lr.at[which], device_id=(j, d), device_id_type=MESH,
-            ).start()
+        def send(along_y, across):
+            y = lax.rem(y_own + along_y, Y_DEV) * X_DEV
+            for dz, dx in across:
+                j = z_base[dz] + y + x_of[dx]
+                pltpu.make_async_remote_copy(
+                    src_ref=sent.at[j], dst_ref=got.at[a], send_sem=ls.at[which],
+                    recv_sem=lr.at[which], device_id=(j, d), device_id_type=MESH,
+                ).start()
+
+        def farther(i, carry):
+            off = (i + 1) // 2
+            send(jnp.where(lax.rem(i, 2) == 1, Y_DEV // 2 - off, Y_DEV // 2 + off), across)
             return carry
 
-        lax.fori_loop(1, LAT_DEV, send, 0, unroll=5)
+        lax.fori_loop(0, Y_DEV - 1, farther, 0)
+        send(0, across[:-1])
         pltpu.make_async_copy(sent, got, lr.at[which]).wait()
 
     all_lat(lat_s1, lat_r1, 0)
@@ -292,22 +296,35 @@
     load_ti.wait()
     modes = lat_r2[...].reshape(COEF, CH)
 
-    def block_of(p):
-        send2[p] = jnp.dot(tiv[p], modes, preferred_element_type=F32).astype(BF16)
-
-    def swap2(k):
-        p = partner(k)
-        return pltpu.make_async_remote_copy(
-            src_ref=send2.at[p], dst_ref=recv2.at[d], send_sem=s2.at[k], recv_sem=r2.at[k],
-            device_id=(a, p), device_id_type=MESH,
-        )
-
-    for k in far_first:
-        block_of(partner(k))
-        swap2(k).start()
-    block_of(d)
+    def block_of(p, half):
+        part = pl.ds(half * HALF, HALF)
+        send2[p, part, :] = jnp.dot(tiv[p, part, :], modes, preferred_element_type=F32).astype(BF16)
+
+    for half in range(2):
+        for k in far_first:
+            block_of(partner(k), half)
+            swap(send2, recv2, s2, r2, half, k).start()
+    for half in range(2):
+        block_of(d, half)
     own2 = pltpu.make_async_copy(send2.at[d], recv2.at[d], own_sem.at[1])
     own2.start()
+
+    load_w.wait()
+    wf[...] = wv[...].astype(F32)
+
+    def weights(step, carry):
+        row, half = step // 2, lax.rem(step, 2)
+        o = pl.multiple_of(half * 64, 64)
+        for t in range(TAPS):
+            total = None
+            for k in range(KINDS):
+                part = wf[k, pl.ds(o, 64), :] * kbc[row, pl.ds(16 * t + k, 1), :]
+                total = part if total is None else total + part
+            tap_row, tap_col = t // 3, t % 3
+            weff[row, pl.ds(tap_col * CH + o, 64), pl.ds(tap_row * CH, CH)] = total.astype(BF16)
+        return carry
+
+    lax.fori_loop(0, 2 * (ROWS + 2), weights, 0)
 
     for copy in edges:
         copy.wait()
@@ -345,18 +362,21 @@
     lax.fori_loop(0, ROWS + 2, stencil, 0)
 
     own2.wait()
-    for k in far_first:
-        swap2(k).wait()
-    for chunk in range(LONP // 16):
-        first = chunk * 16
-        blocks = [recv2[e, pl.ds(first, 16), :].astype(F32) for e in range(LON_DEV)]
-        rows = exchange_groups(blocks, group16)
-        for r in range(ROWS):
-            total = dsum[r + 2, pl.ds(first, 16), :]
-            total = total + rows[r] * qw_ref[a * ROWS + r]
-            total = jnp.where(r < live, total, 0.0)
-            outf[pl.ds(first * ROWS + r, 16, stride=ROWS), :] = total
-    out_ref[...] = outf[pl.ds(0, LON * ROWS), :].astype(BF16).reshape(LON, ROWS, CH)
+    for half in range(2):
+        for k in far_first:
+            swap(send2, recv2, s2, r2, half, k).wait()
+        for chunk in range(HALF // 16):
+            first = half * HALF + chunk * 16
+            blocks = [recv2[e, pl.ds(first, 16), :].astype(F32) for e in range(LON_DEV)]
+            rows = exchange_groups(blocks, group16)
+            for r in range(ROWS):
+                total = dsum[r + 2, pl.ds(first, 16), :]
+                total = total + rows[r] * qw_ref[a * ROWS + r]
+                total = jnp.where(r < live, total, 0.0)
+                outf[pl.ds(first * ROWS + r, 16, stride=ROWS), :] = total
+        count = HALF if half == 0 else LON - HALF
+        done = outf[pl.ds(half * HALF * ROWS, count * ROWS), :].astype(BF16)
+        out_ref[pl.ds(half * HALF, count)] = done.reshape(count, ROWS, CH)
 
     for which, sent in ((0, lat_s1), (1, lat_s2)):
         most = sent.at[pl.ds(0, LAT_DEV - 1)]
@@ -410,10 +430,10 @@
             vmem((LONP * ROWS, CH), F32),
             dma((8,)),
             dma((2,)),
-            dma((8,)),
-            dma((8,)),
-            dma((8,)),
-            dma((8,)),
+            dma((2, 8)),
+            dma((2, 8)),
+            dma((2, 8)),
+            dma((2, 8)),
             dma((8,)),
             dma((8,)),
             dma((2,)),

time: 75.2 us -> 74.4 us (0.989)
  Pallas kernels: 73.2 us -> 72.4 us
    pallas_call x1, Pallas kernels: 73.2 us -> 72.4 us  [on_device(): pl.pallas_call(kernel, out_shape=jax.ShapeDtypeStruct((LON, ROWS, CH), BF...]
where the time goes in v2:
time: 74.4 us; the launch traced here: 74.2 us
  Pallas kernels  72.4 us (97%)
  local copies, waits for them, and re-layouts  1.75 us (2%)
    pallas_call x1, Pallas kernels, on_device(): pl.pallas_call(kernel, out_shape=jax.ShapeDtypeStruct((LON, ROWS, CH), BF...  72.4 us
    unnamed x1, local copies, waits for them, and re-layouts  1.75 us

profile of v2, /device:TPU:1, one launch (start us, length us, event | category | flops | bytes accessed | tf_op | source)
XLA Modules:
  0.0 74.2 jit_solution(5161974987284201636)
XLA Ops:
  0.0 72.4 %shard_map.91 = bf16[180,8,128]{2,1,0:T(8,128)(2,1)} custom-call(s32[96]{0:T(128)} %rows_ref.1, f32[768]{0:T(1024)} %qw_ref.1, bf16[180,8,128]{2,1,0:T(8,128)(2,1)} %bitcast.6, f32[2,360,768]{2,1,0:T(8,128)} %leg_ref.1, f32[2,360,128]{2,1,0:T(8,128)} %filt_ref.1, f32[9,9,768]{2,1,0:T(8,128)} %bitcast.5, bf16[9,128,128]{2,1,0:T(8,128)(2,1)} %bitcast.7, ...), custom_call_target="tpu_custom_call" | custom-call | tf_op jit(solution)/shard_map/pallas_call | solution.py:391
  72.5 1.7 %copy.11 = bf16[8,180,128]{2,0,1:T(8,128)(2,1)} copy(bf16[8,180,128]{2,0,1:T(8,128)(2,1)} %bitcast.4) | data formatting | bytes 737280

commit v3 on v2

--- a/solution.py
+++ b/solution.py
@@ -38,9 +38,10 @@
     table = np.stack([np.cos(angle), -np.sin(angle)], axis=2) * points**-0.5
     blocks = np.zeros((LON_DEV, LONP, COEF))
     blocks[:, :LON] = table.reshape(LON_DEV, LON, COEF)
-    inverse = blocks.astype(ml_dtypes.bfloat16)
-    forward = np.ascontiguousarray(inverse.reshape(LON_DEV * LONP, COEF).T)
-    return forward, inverse
+    parts = blocks.astype(ml_dtypes.bfloat16).reshape(LON_DEV, 2, HALF, LAT_DEV, 2, 2)
+    forward = parts.transpose(1, 4, 3, 5, 0, 2).reshape(2, COEF, LON_DEV * HALF)
+    inverse = parts.transpose(0, 1, 4, 2, 3, 5).reshape(LON_DEV, 4 * HALF, MODES)
+    return np.ascontiguousarray(forward), np.ascontiguousarray(inverse)
 
 
 def exchange_groups(rows, group_bit):
@@ -113,11 +114,15 @@
 
     far_first = (4, 5, 2, 6, 3, 7, 1)
 
+    def low_half(count):
+        return (lax.broadcasted_iota(jnp.int32, (count, CH), 1) & 8) == 0
+
+    low16 = low_half(16)
+
     def swap(sent, got, send_sem, recv_sem, half, k):
         p = partner(k)
-        part = pl.ds(half * HALF, HALF)
         return pltpu.make_async_remote_copy(
-            src_ref=sent.at[p, part], dst_ref=got.at[d, part], send_sem=send_sem.at[half, k],
+            src_ref=sent.at[half, p], dst_ref=got.at[half, d], send_sem=send_sem.at[half, k],
             recv_sem=recv_sem.at[half, k], device_id=(a, p), device_id_type=MESH,
         )
 
@@ -129,18 +134,27 @@
         xf[pl.ds(half * HALF * ROWS, count * ROWS), :] = masked.reshape(count * ROWS, CH)
         if half == 1:
             xf[pl.ds(LON * ROWS, (LONP - LON) * ROWS), :] = jnp.zeros(((LONP - LON) * ROWS, CH), F32)
-        for chunk in range(HALF // 16):
-            first = half * HALF + chunk * 16
-            rows = [xf[pl.ds(first * ROWS + r, 16, stride=ROWS), :] for r in range(ROWS)]
-            swapped = exchange_groups(rows, group16)
-            for p in range(LON_DEV):
-                send1[p, pl.ds(first, 16), :] = swapped[p].astype(BF16)
-        if half == 0:
-            pl.semaphore_wait(barrier, LAT_DEV - 1 + LON_DEV - 1 + 4)
+
+    for chunk in range(HALF // 16):
+        first = chunk * 16
+        both = []
+        for start in (first, first + HALF):
+            rows = [xf[pl.ds(start * ROWS + r, 16, stride=ROWS), :] for r in range(ROWS)]
+            both.append(exchange_groups(rows, group16))
+        for p in range(LON_DEV):
+            one, two = both[0][p], both[1][p]
+            send1[0, p, pl.ds(first, 16), :] = jnp.where(low16, one, pltpu.roll(two, 8, 1)).astype(BF16)
+            send1[1, p, pl.ds(first, 16), :] = jnp.where(low16, pltpu.roll(one, CH - 8, 1), two).astype(BF16)
+    pl.semaphore_wait(barrier, LAT_DEV - 1 + LON_DEV - 1 + 4)
+    for half in range(2):
         for k in far_first:
             swap(send1, recv1, s1, r1, half, k).start()
-    own1 = pltpu.make_async_copy(send1.at[d], recv1.at[d], own_sem.at[0])
-    own1.start()
+    own1 = [
+        pltpu.make_async_copy(send1.at[half, d], recv1.at[half, d], own_sem.at[half])
+        for half in range(2)
+    ]
+    for copy in own1:
+        copy.start()
 
     for r in range(ROWS):
         row = xf[pl.ds(r, LONP, stride=ROWS), :]
@@ -200,11 +214,12 @@
     lane = lax.broadcasted_iota(jnp.int32, (DEG, CH), 1)
     filtr[...] = jnp.zeros_like(filtr)
     for part in range(2):
-        mine = pltpu.roll(filtv[part], lax.rem(CH - SHARE * d, CH), 1)
-        mine = jnp.where(lane < SHARE, mine, 0.0)
-        for step in (SHARE, 2 * SHARE, 4 * SHARE):
-            mine = mine + pltpu.roll(mine, step, 1)
-        filtr[part, pl.ds(0, DEG), :] = mine
+        for half in range(2):
+            mine = pltpu.roll(filtv[part], lax.rem(2 * CH - SHARE * d - 8 * half, CH), 1)
+            mine = jnp.where(lane < 8, mine, 0.0)
+            for step in (8, 16, 32, 64):
+                mine = mine + pltpu.roll(mine, step, 1)
+            filtr[half, part, pl.ds(0, DEG), :] = mine
 
     band_row = lax.broadcasted_iota(jnp.int32, (LAT_DEV, SLOTS), 0)
     band_col = lax.broadcasted_iota(jnp.int32, (LAT_DEV, SLOTS), 1) // ROWS
@@ -224,16 +239,7 @@
     for row in range(ROWS + 2):
         kbc[row] = jnp.broadcast_to(chosen[:, row : row + 1], (16 * TAPS, CH))
 
-    own1.wait()
-    for half in range(2):
-        for k in far_first:
-            swap(send1, recv1, s1, r1, half, k).wait()
     load_tf.wait()
-    spectra = jnp.dot(
-        tfv[...], recv1[...].reshape(LON_DEV * LONP, CH), preferred_element_type=F32
-    )
-    lat_s1[...] = spectra.astype(BF16).reshape(LAT_DEV, 4, CH)
-
     x_own, y_own, z_own = lax.rem(a, X_DEV), lax.rem(a // X_DEV, Y_DEV), a // (X_DEV * Y_DEV)
     x_of = [lax.rem(x_own + dx, X_DEV) for dx in range(X_DEV)]
     z_base = [lax.rem(z_own + dz, Z_DEV) * (X_DEV * Y_DEV) for dz in range(Z_DEV)]
@@ -259,20 +265,38 @@
 
         lax.fori_loop(0, Y_DEV - 1, farther, 0)
         send(0, across[:-1])
-        pltpu.make_async_copy(sent, got, lr.at[which]).wait()
-
-    all_lat(lat_s1, lat_r1, 0)
-
-    coltmp[...] = lat_r1[...].astype(F32).reshape(COEF, CH)
+
+    low_rows = low_half(MODES)
+    for half in range(2):
+        own1[half].wait()
+        for k in far_first:
+            swap(send1, recv1, s1, r1, half, k).wait()
+        field = recv1[half].reshape(LON_DEV * HALF, CH)
+        one = jnp.dot(tfv[0], field, preferred_element_type=F32)
+        two = jnp.dot(tfv[1], field, preferred_element_type=F32)
+        even = one[:MODES] + pltpu.roll(two[:MODES], CH - 8, 1)
+        odd = pltpu.roll(one[MODES:], 8, 1) + two[MODES:]
+        spectra = jnp.where(low_rows, even, odd).astype(BF16)
+        lat_s1[half] = spectra.reshape(LAT_DEV, 2, CH)
+        all_lat(lat_s1.at[half], lat_r1.at[half], half)
+
     block_slot = lax.broadcasted_iota(jnp.int32, (LAT_DEV, ROWS, CH), 1)
-    block_group = lax.broadcasted_iota(jnp.int32, (LAT_DEV, ROWS, CH), 2) // SHARE
-    diagonal = block_slot == block_group
-    for q in range(4):
-        column = coltmp[pl.ds(q, LAT_DEV, stride=4), :]
-        wide = jnp.where(diagonal, column[:, None, :], 0.0)
-        rhs[:, pl.ds(q * CH, CH)] = wide.reshape(SLOTS, CH).astype(BF16)
-    for mm in range(2):
-        coef = jnp.dot(legb[mm], rhs[:, pl.ds(mm * 2 * CH, 2 * CH)], preferred_element_type=F32)
+    block_lane = lax.broadcasted_iota(jnp.int32, (LAT_DEV, ROWS, CH), 2)
+    diagonal = block_slot == block_lane // SHARE
+    low_slots = (lax.broadcasted_iota(jnp.int32, (SLOTS, 2 * CH), 1) & 8) == 0
+    low_degrees = (lax.broadcasted_iota(jnp.int32, (DEGP, 2 * CH), 1) & 8) == 0
+    for half in range(2):
+        pltpu.make_async_copy(lat_s1.at[half], lat_r1.at[half], lr.at[half]).wait()
+        coltmp[half] = lat_r1[half].astype(F32).reshape(2 * LAT_DEV, CH)
+        for q in range(2):
+            column = coltmp[half, pl.ds(q, LAT_DEV, stride=2), :]
+            wide = jnp.where(diagonal, column[:, None, :], 0.0)
+            rhs[half, :, pl.ds(q * CH, CH)] = wide.reshape(SLOTS, CH).astype(BF16)
+        coef = jnp.where(
+            low_degrees,
+            jnp.dot(legb[0], rhs[half], preferred_element_type=F32),
+            jnp.dot(legb[1], rhs[half], preferred_element_type=F32),
+        )
         parts = []
         for part in range(2):
             folded = coef[:, part * CH : (part + 1) * CH]
@@ -280,34 +304,44 @@
                 folded = folded + pltpu.roll(folded, step, 1)
             parts.append(folded)
         real, imag = parts
-        fr, fi = filtr[0], filtr[1]
-        filtered = jnp.concatenate([fr * real + fi * imag, fr * imag - fi * real], axis=1)
-        back = jnp.dot(legt[mm], filtered.astype(BF16), preferred_element_type=F32)
+        fr, fi = filtr[half, 0], filtr[half, 1]
+        filtered = jnp.concatenate([fr * real + fi * imag, fr * imag - fi * real], axis=1).astype(BF16)
+        back = jnp.where(
+            low_slots,
+            jnp.dot(legt[0], filtered, preferred_element_type=F32),
+            jnp.dot(legt[1], filtered, preferred_element_type=F32),
+        )
         for part in range(2):
             wide = back[:, part * CH : (part + 1) * CH].reshape(LAT_DEV, ROWS, CH)
             wide = jnp.where(diagonal, wide, 0.0).astype(BF16)
-            zed[:, pl.ds((2 * mm + part) * CH, CH)] = wide.reshape(SLOTS, CH)
-    returned = jnp.dot(pick[...], zed[...], preferred_element_type=F32)
-    for q in range(4):
-        coltmp[pl.ds(q, LAT_DEV, stride=4), :] = returned[:, q * CH : (q + 1) * CH]
-    lat_s2[...] = coltmp[...].astype(BF16).reshape(LAT_DEV, 4, CH)
-    all_lat(lat_s2, lat_r2, 1)
+            zed[half, :, pl.ds(part * CH, CH)] = wide.reshape(SLOTS, CH)
+        returned = jnp.dot(pick[...], zed[half], preferred_element_type=F32)
+        for q in range(2):
+            coltmp[half, pl.ds(q, LAT_DEV, stride=2), :] = returned[:, q * CH : (q + 1) * CH]
+        lat_s2[half] = coltmp[half].astype(BF16).reshape(LAT_DEV, 2, CH)
+        all_lat(lat_s2.at[half], lat_r2.at[half], 2 + half)
 
     load_ti.wait()
-    modes = lat_r2[...].reshape(COEF, CH)
-
-    def block_of(p, half):
-        part = pl.ds(half * HALF, HALF)
-        send2[p, part, :] = jnp.dot(tiv[p, part, :], modes, preferred_element_type=F32).astype(BF16)
-
-    for half in range(2):
+    low_block = low_half(HALF)
+
+    def block_of(p, half, modes):
+        four = jnp.dot(tiv[p], modes, preferred_element_type=F32)
+        first = four[:HALF] + pltpu.roll(four[HALF : 2 * HALF], CH - 8, 1)
+        second = pltpu.roll(four[2 * HALF : 3 * HALF], 8, 1) + four[3 * HALF :]
+        send2[half, p] = jnp.where(low_block, first, second).astype(BF16)
+
+    own2 = []
+    for half in range(2):
+        pltpu.make_async_copy(lat_s2.at[half], lat_r2.at[half], lr.at[2 + half]).wait()
+        modes = lat_r2[half].reshape(MODES, CH)
         for k in far_first:
-            block_of(partner(k), half)
+            block_of(partner(k), half, modes)
             swap(send2, recv2, s2, r2, half, k).start()
-    for half in range(2):
-        block_of(d, half)
-    own2 = pltpu.make_async_copy(send2.at[d], recv2.at[d], own_sem.at[1])
-    own2.start()
+        block_of(d, half, modes)
+        own2.append(
+            pltpu.make_async_copy(send2.at[half, d], recv2.at[half, d], own_sem.at[2 + half])
+        )
+        own2[half].start()
 
     load_w.wait()
     wf[...] = wv[...].astype(F32)
@@ -361,26 +395,32 @@
 
     lax.fori_loop(0, ROWS + 2, stencil, 0)
 
-    own2.wait()
-    for half in range(2):
+    for half in range(2):
+        own2[half].wait()
         for k in far_first:
             swap(send2, recv2, s2, r2, half, k).wait()
-        for chunk in range(HALF // 16):
-            first = half * HALF + chunk * 16
-            blocks = [recv2[e, pl.ds(first, 16), :].astype(F32) for e in range(LON_DEV)]
-            rows = exchange_groups(blocks, group16)
+    for chunk in range(HALF // 16):
+        begin = chunk * 16
+        blocks = ([], [])
+        for e in range(LON_DEV):
+            one = recv2[0, e, pl.ds(begin, 16), :].astype(F32)
+            two = recv2[1, e, pl.ds(begin, 16), :].astype(F32)
+            blocks[0].append(jnp.where(low16, one, pltpu.roll(two, 8, 1)))
+            blocks[1].append(jnp.where(low16, pltpu.roll(one, CH - 8, 1), two))
+        for half in range(2):
+            first = half * HALF + begin
+            rows = exchange_groups(blocks[half], group16)
             for r in range(ROWS):
                 total = dsum[r + 2, pl.ds(first, 16), :]
                 total = total + rows[r] * qw_ref[a * ROWS + r]
                 total = jnp.where(r < live, total, 0.0)
                 outf[pl.ds(first * ROWS + r, 16, stride=ROWS), :] = total
-        count = HALF if half == 0 else LON - HALF
-        done = outf[pl.ds(half * HALF * ROWS, count * ROWS), :].astype(BF16)
-        out_ref[pl.ds(half * HALF, count)] = done.reshape(count, ROWS, CH)
-
-    for which, sent in ((0, lat_s1), (1, lat_s2)):
-        most = sent.at[pl.ds(0, LAT_DEV - 1)]
-        pltpu.make_async_copy(most, most, ls.at[which]).wait()
+    out_ref[...] = outf[pl.ds(0, LON * ROWS), :].astype(BF16).reshape(LON, ROWS, CH)
+
+    for half in range(2):
+        for which, sent in ((half, lat_s1), (2 + half, lat_s2)):
+            most = sent.at[half, pl.ds(0, LAT_DEV - 1)]
+            pltpu.make_async_copy(most, most, ls.at[which]).wait()
 
 
 def on_device(grad_output, band_rows, legendre, quad_weights, spectral_filter, disco_kernel, disco_weight):
@@ -397,14 +437,14 @@
             vmem((LON, ROWS, CH), BF16),
             vmem((LONP * ROWS, CH), F32),
             vmem((ROWS + 2, LONP + 2 * EDGE, CH), F32),
-            vmem((LON_DEV, LONP, CH), BF16),
-            vmem((LON_DEV, LONP, CH), BF16),
-            vmem((LAT_DEV, 4, CH), BF16),
-            vmem((LAT_DEV, 4, CH), BF16),
-            vmem((LAT_DEV, 4, CH), BF16),
-            vmem((LAT_DEV, 4, CH), BF16),
-            vmem((LON_DEV, LONP, CH), BF16),
-            vmem((LON_DEV, LONP, CH), BF16),
+            vmem((2, LON_DEV, HALF, CH), BF16),
+            vmem((2, LON_DEV, HALF, CH), BF16),
+            vmem((2, LAT_DEV, 2, CH), BF16),
+            vmem((2, LAT_DEV, 2, CH), BF16),
+            vmem((2, LAT_DEV, 2, CH), BF16),
+            vmem((2, LAT_DEV, 2, CH), BF16),
+            vmem((2, LON_DEV, HALF, CH), BF16),
+            vmem((2, LON_DEV, HALF, CH), BF16),
             vmem((2, LONP, CH), BF16),
             vmem((2, LONP, CH), BF16),
             vmem((6, 16, CH), BF16),
@@ -413,31 +453,31 @@
             vmem((2, DEGP, SLOTS), BF16),
             vmem((2, SLOTS, DEGP), BF16),
             vmem((2, DEG, CH), F32),
-            vmem((2, DEGP, CH), F32),
+            vmem((2, 2, DEGP, CH), F32),
             vmem((TAPS, KINDS, SLOTS), F32),
             vmem((16 * TAPS, SLOTS), F32),
             vmem((ROWS + 2, 16 * TAPS, CH), F32),
             vmem((KINDS, CH, CH), BF16),
             vmem((KINDS, CH, CH), F32),
             vmem((ROWS + 2, 3 * CH, 3 * CH), BF16),
-            vmem((COEF, LON_DEV * LONP), BF16),
-            vmem((LON_DEV, LONP, COEF), BF16),
+            vmem((2, COEF, LON_DEV * HALF), BF16),
+            vmem((LON_DEV, 4 * HALF, MODES), BF16),
             vmem((ROWS + 4, LONP, CH), F32),
-            vmem((COEF, CH), F32),
-            vmem((SLOTS, 4 * CH), BF16),
-            vmem((SLOTS, 4 * CH), BF16),
+            vmem((2, 2 * LAT_DEV, CH), F32),
+            vmem((2, SLOTS, 2 * CH), BF16),
+            vmem((2, SLOTS, 2 * CH), BF16),
             vmem((LAT_DEV, SLOTS), BF16),
             vmem((LONP * ROWS, CH), F32),
             dma((8,)),
-            dma((2,)),
+            dma((4,)),
             dma((2, 8)),
             dma((2, 8)),
             dma((2, 8)),
             dma((2, 8)),
             dma((8,)),
             dma((8,)),
-            dma((2,)),
-            dma((2,)),
+            dma((4,)),
+            dma((4,)),
         ],
         compiler_params=pltpu.CompilerParams(
             collective_id=0, has_side_effects=True, vmem_limit_bytes=56 * 2**20

time: 74.4 us -> 70.3 us (0.945); the launches traced: 74.2 us -> 69.1 us
  Pallas kernels: 72.4 us -> 67.3 us
    pallas_call x1, Pallas kernels: 72.4 us -> 67.3 us  [on_device(): pl.pallas_call(kernel, out_shape=jax.ShapeDtypeStruct((LON, ROWS, CH), BF...]
where the time goes in v3:
time: 70.3 us; the launch traced here: 69.1 us
  Pallas kernels  67.3 us (96%)
  local copies, waits for them, and re-layouts  1.75 us (2%)
    pallas_call x1, Pallas kernels, on_device(): pl.pallas_call(kernel, out_shape=jax.ShapeDtypeStruct((LON, ROWS, CH), BF...  67.3 us
    unnamed x1, local copies, waits for them, and re-layouts  1.75 us

profile of v3, /device:TPU:1, one launch (start us, length us, event | category | flops | bytes accessed | tf_op | source)
XLA Modules:
  0.0 69.1 jit_solution(7211757267920658995)
XLA Ops:
  0.0 67.3 %shard_map.91 = bf16[180,8,128]{2,1,0:T(8,128)(2,1)} custom-call(s32[96]{0:T(128)} %rows_ref.1, f32[768]{0:T(1024)} %qw_ref.1, bf16[180,8,128]{2,1,0:T(8,128)(2,1)} %bitcast.6, f32[2,360,768]{2,1,0:T(8,128)} %leg_ref.1, f32[2,360,128]{2,1,0:T(8,128)} %filt_ref.1, f32[9,9,768]{2,1,0:T(8,128)} %bitcast.5, bf16[9,128,128]{2,1,0:T(8,128)(2,1)} %bitcast.7, ...), custom_call_target="tpu_custom_call" | custom-call | tf_op jit(solution)/shard_map/pallas_call | solution.py:431
  67.3 1.7 %copy.11 = bf16[8,180,128]{2,0,1:T(8,128)(2,1)} copy(bf16[8,180,128]{2,0,1:T(8,128)(2,1)} %bitcast.4) | data formatting | bytes 737280

commit v4 on v3

--- a/solution.py
+++ b/solution.py
@@ -225,6 +225,110 @@
     band_col = lax.broadcasted_iota(jnp.int32, (LAT_DEV, SLOTS), 1) // ROWS
     pick[...] = jnp.where(band_row == band_col, 1.0, 0.0).astype(BF16)
 
+    load_tf.wait()
+    x_own, y_own, z_own = lax.rem(a, X_DEV), lax.rem(a // X_DEV, Y_DEV), a // (X_DEV * Y_DEV)
+    x_of = [lax.rem(x_own + dx, X_DEV) for dx in range(X_DEV)]
+    z_base = [lax.rem(z_own + dz, Z_DEV) * (X_DEV * Y_DEV) for dz in range(Z_DEV)]
+    across = [(dz, dx) for dz in (1, 2, 0) for dx in (2, 1, 3, 0)]
+
+    def all_lat(sent, got, which):
+        own = pltpu.make_async_copy(sent.at[a], got.at[a], lr.at[which])
+        own.start()
+
+        def send(along_y, across):
+            y = lax.rem(y_own + along_y, Y_DEV) * X_DEV
+            for dz, dx in across:
+                j = z_base[dz] + y + x_of[dx]
+                pltpu.make_async_remote_copy(
+                    src_ref=sent.at[j], dst_ref=got.at[a], send_sem=ls.at[which],
+                    recv_sem=lr.at[which], device_id=(j, d), device_id_type=MESH,
+                ).start()
+
+        def farther(i, carry):
+            off = (i + 1) // 2
+            send(jnp.where(lax.rem(i, 2) == 1, Y_DEV // 2 - off, Y_DEV // 2 + off), across)
+            return carry
+
+        lax.fori_loop(0, Y_DEV - 1, farther, 0)
+        send(0, across[:-1])
+
+    low_rows = low_half(MODES)
+    for half in range(2):
+        own1[half].wait()
+        for k in far_first:
+            swap(send1, recv1, s1, r1, half, k).wait()
+        field = recv1[half].reshape(LON_DEV * HALF, CH)
+        one = jnp.dot(tfv[0], field, preferred_element_type=F32)
+        two = jnp.dot(tfv[1], field, preferred_element_type=F32)
+        even = one[:MODES] + pltpu.roll(two[:MODES], CH - 8, 1)
+        odd = pltpu.roll(one[MODES:], 8, 1) + two[MODES:]
+        spectra = jnp.where(low_rows, even, odd).astype(BF16)
+        lat_s1[half] = spectra.reshape(LAT_DEV, 2, CH)
+        all_lat(lat_s1.at[half], lat_r1.at[half], half)
+
+    block_slot = lax.broadcasted_iota(jnp.int32, (LAT_DEV, ROWS, CH), 1)
+    block_lane = lax.broadcasted_iota(jnp.int32, (LAT_DEV, ROWS, CH), 2)
+    diagonal = block_slot == block_lane // SHARE
+    low_slots = (lax.broadcasted_iota(jnp.int32, (SLOTS, 2 * CH), 1) & 8) == 0
+    low_degrees = (lax.broadcasted_iota(jnp.int32, (DEGP, 2 * CH), 1) & 8) == 0
+    for half in range(2):
+        pltpu.make_async_copy(lat_s1.at[half], lat_r1.at[half], lr.at[half]).wait()
+        coltmp[half] = lat_r1[half].astype(F32).reshape(2 * LAT_DEV, CH)
+        for q in range(2):
+            column = coltmp[half, pl.ds(q, LAT_DEV, stride=2), :]
+            wide = jnp.where(diagonal, column[:, None, :], 0.0)
+            rhs[half, :, pl.ds(q * CH, CH)] = wide.reshape(SLOTS, CH).astype(BF16)
+        coef = jnp.where(
+            low_degrees,
+            jnp.dot(legb[0], rhs[half], preferred_element_type=F32),
+            jnp.dot(legb[1], rhs[half], preferred_element_type=F32),
+        )
+        parts = []
+        for part in range(2):
+            folded = coef[:, part * CH : (part + 1) * CH]
+            for step in (SHARE, 2 * SHARE, 4 * SHARE):
+                folded = folded + pltpu.roll(folded, step, 1)
+            parts.append(folded)
+        real, imag = parts
+        fr, fi = filtr[half, 0], filtr[half, 1]
+        filtered = jnp.concatenate([fr * real + fi * imag, fr * imag - fi * real], axis=1).astype(BF16)
+        back = jnp.where(
+            low_slots,
+            jnp.dot(legt[0], filtered, preferred_element_type=F32),
+            jnp.dot(legt[1], filtered, preferred_element_type=F32),
+        )
+        for part in range(2):
+            wide = back[:, part * CH : (part + 1) * CH].reshape(LAT_DEV, ROWS, CH)
+            wide = jnp.where(diagonal, wide, 0.0).astype(BF16)
+            zed[half, :, pl.ds(part * CH, CH)] = wide.reshape(SLOTS, CH)
+        returned = jnp.dot(pick[...], zed[half], preferred_element_type=F32)
+        for q in range(2):
+            coltmp[half, pl.ds(q, LAT_DEV, stride=2), :] = returned[:, q * CH : (q + 1) * CH]
+        lat_s2[half] = coltmp[half].astype(BF16).reshape(LAT_DEV, 2, CH)
+        all_lat(lat_s2.at[half], lat_r2.at[half], 2 + half)
+
+    load_ti.wait()
+    low_block = low_half(HALF)
+
+    def block_of(p, half, modes):
+        four = jnp.dot(tiv[p], modes, preferred_element_type=F32)
+        first = four[:HALF] + pltpu.roll(four[HALF : 2 * HALF], CH - 8, 1)
+        second = pltpu.roll(four[2 * HALF : 3 * HALF], 8, 1) + four[3 * HALF :]
+        send2[half, p] = jnp.where(low_block, first, second).astype(BF16)
+
+    own2 = []
+    for half in range(2):
+        pltpu.make_async_copy(lat_s2.at[half], lat_r2.at[half], lr.at[2 + half]).wait()
+        modes = lat_r2[half].reshape(MODES, CH)
+        for k in far_first:
+            block_of(partner(k), half, modes)
+            swap(send2, recv2, s2, r2, half, k).start()
+        block_of(d, half, modes)
+        own2.append(
+            pltpu.make_async_copy(send2.at[half, d], recv2.at[half, d], own_sem.at[2 + half])
+        )
+        own2[half].start()
+
     load_kern.wait()
     kpad[...] = jnp.zeros_like(kpad)
     for t in range(TAPS):
@@ -238,110 +342,6 @@
     chosen = jnp.dot(kpad[...], one_hot, precision=lax.Precision.HIGHEST, preferred_element_type=F32)
     for row in range(ROWS + 2):
         kbc[row] = jnp.broadcast_to(chosen[:, row : row + 1], (16 * TAPS, CH))
-
-    load_tf.wait()
-    x_own, y_own, z_own = lax.rem(a, X_DEV), lax.rem(a // X_DEV, Y_DEV), a // (X_DEV * Y_DEV)
-    x_of = [lax.rem(x_own + dx, X_DEV) for dx in range(X_DEV)]
-    z_base = [lax.rem(z_own + dz, Z_DEV) * (X_DEV * Y_DEV) for dz in range(Z_DEV)]
-    across = [(dz, dx) for dz in (1, 2, 0) for dx in (2, 1, 3, 0)]
-
-    def all_lat(sent, got, which):
-        own = pltpu.make_async_copy(sent.at[a], got.at[a], lr.at[which])
-        own.start()
-
-        def send(along_y, across):
-            y = lax.rem(y_own + along_y, Y_DEV) * X_DEV
-            for dz, dx in across:
-                j = z_base[dz] + y + x_of[dx]
-                pltpu.make_async_remote_copy(
-                    src_ref=sent.at[j], dst_ref=got.at[a], send_sem=ls.at[which],
-                    recv_sem=lr.at[which], device_id=(j, d), device_id_type=MESH,
-                ).start()
-
-        def farther(i, carry):
-            off = (i + 1) // 2
-            send(jnp.where(lax.rem(i, 2) == 1, Y_DEV // 2 - off, Y_DEV // 2 + off), across)
-            return carry
-
-        lax.fori_loop(0, Y_DEV - 1, farther, 0)
-        send(0, across[:-1])
-
-    low_rows = low_half(MODES)
-    for half in range(2):
-        own1[half].wait()
-        for k in far_first:
-            swap(send1, recv1, s1, r1, half, k).wait()
-        field = recv1[half].reshape(LON_DEV * HALF, CH)
-        one = jnp.dot(tfv[0], field, preferred_element_type=F32)
-        two = jnp.dot(tfv[1], field, preferred_element_type=F32)
-        even = one[:MODES] + pltpu.roll(two[:MODES], CH - 8, 1)
-        odd = pltpu.roll(one[MODES:], 8, 1) + two[MODES:]
-        spectra = jnp.where(low_rows, even, odd).astype(BF16)
-        lat_s1[half] = spectra.reshape(LAT_DEV, 2, CH)
-        all_lat(lat_s1.at[half], lat_r1.at[half], half)
-
-    block_slot = lax.broadcasted_iota(jnp.int32, (LAT_DEV, ROWS, CH), 1)
-    block_lane = lax.broadcasted_iota(jnp.int32, (LAT_DEV, ROWS, CH), 2)
-    diagonal = block_slot == block_lane // SHARE
-    low_slots = (lax.broadcasted_iota(jnp.int32, (SLOTS, 2 * CH), 1) & 8) == 0
-    low_degrees = (lax.broadcasted_iota(jnp.int32, (DEGP, 2 * CH), 1) & 8) == 0
-    for half in range(2):
-        pltpu.make_async_copy(lat_s1.at[half], lat_r1.at[half], lr.at[half]).wait()
-        coltmp[half] = lat_r1[half].astype(F32).reshape(2 * LAT_DEV, CH)
-        for q in range(2):
-            column = coltmp[half, pl.ds(q, LAT_DEV, stride=2), :]
-            wide = jnp.where(diagonal, column[:, None, :], 0.0)
-            rhs[half, :, pl.ds(q * CH, CH)] = wide.reshape(SLOTS, CH).astype(BF16)
-        coef = jnp.where(
-            low_degrees,
-            jnp.dot(legb[0], rhs[half], preferred_element_type=F32),
-            jnp.dot(legb[1], rhs[half], preferred_element_type=F32),
-        )
-        parts = []
-        for part in range(2):
-            folded = coef[:, part * CH : (part + 1) * CH]
-            for step in (SHARE, 2 * SHARE, 4 * SHARE):
-                folded = folded + pltpu.roll(folded, step, 1)
-            parts.append(folded)
-        real, imag = parts
-        fr, fi = filtr[half, 0], filtr[half, 1]
-        filtered = jnp.concatenate([fr * real + fi * imag, fr * imag - fi * real], axis=1).astype(BF16)
-        back = jnp.where(
-            low_slots,
-            jnp.dot(legt[0], filtered, preferred_element_type=F32),
-            jnp.dot(legt[1], filtered, preferred_element_type=F32),
-        )
-        for part in range(2):
-            wide = back[:, part * CH : (part + 1) * CH].reshape(LAT_DEV, ROWS, CH)
-            wide = jnp.where(diagonal, wide, 0.0).astype(BF16)
-            zed[half, :, pl.ds(part * CH, CH)] = wide.reshape(SLOTS, CH)
-        returned = jnp.dot(pick[...], zed[half], preferred_element_type=F32)
-        for q in range(2):
-            coltmp[half, pl.ds(q, LAT_DEV, stride=2), :] = returned[:, q * CH : (q + 1) * CH]
-        lat_s2[half] = coltmp[half].astype(BF16).reshape(LAT_DEV, 2, CH)
-        all_lat(lat_s2.at[half], lat_r2.at[half], 2 + half)
-
-    load_ti.wait()
-    low_block = low_half(HALF)
-
-    def block_of(p, half, modes):
-        four = jnp.dot(tiv[p], modes, preferred_element_type=F32)
-        first = four[:HALF] + pltpu.roll(four[HALF : 2 * HALF], CH - 8, 1)
-        second = pltpu.roll(four[2 * HALF : 3 * HALF], 8, 1) + four[3 * HALF :]
-        send2[half, p] = jnp.where(low_block, first, second).astype(BF16)
-
-    own2 = []
-    for half in range(2):
-        pltpu.make_async_copy(lat_s2.at[half], lat_r2.at[half], lr.at[2 + half]).wait()
-        modes = lat_r2[half].reshape(MODES, CH)
-        for k in far_first:
-            block_of(partner(k), half, modes)
-            swap(send2, recv2, s2, r2, half, k).start()
-        block_of(d, half, modes)
-        own2.append(
-            pltpu.make_async_copy(send2.at[half, d], recv2.at[half, d], own_sem.at[2 + half])
-        )
-        own2[half].start()
 
     load_w.wait()
     wf[...] = wv[...].astype(F32)

time: 70.3 us -> 70.4 us (level)
  no operation moved by 1% of the time
where the time goes in v4:
time: 70.4 us; the launch traced here: 69.4 us
  Pallas kernels  67.6 us (96%)
  local copies, waits for them, and re-layouts  1.75 us (2%)
    pallas_call x1, Pallas kernels, on_device(): pl.pallas_call(kernel, out_shape=jax.ShapeDtypeStruct((LON, ROWS, CH), BF...  67.6 us
    unnamed x1, local copies, waits for them, and re-layouts  1.75 us

profile of v4, /device:TPU:1, one launch (start us, length us, event | category | flops | bytes accessed | tf_op | source)
XLA Modules:
  0.0 69.4 jit_solution(1567048082032340866)
XLA Ops:
  0.0 67.6 %shard_map.91 = bf16[180,8,128]{2,1,0:T(8,128)(2,1)} custom-call(s32[96]{0:T(128)} %rows_ref.1, f32[768]{0:T(1024)} %qw_ref.1, bf16[180,8,128]{2,1,0:T(8,128)(2,1)} %bitcast.6, f32[2,360,768]{2,1,0:T(8,128)} %leg_ref.1, f32[2,360,128]{2,1,0:T(8,128)} %filt_ref.1, f32[9,9,768]{2,1,0:T(8,128)} %bitcast.5, bf16[9,128,128]{2,1,0:T(8,128)(2,1)} %bitcast.7, ...), custom_call_target="tpu_custom_call" | custom-call | tf_op jit(solution)/shard_map/pallas_call | solution.py:431
  67.6 1.7 %copy.11 = bf16[8,180,128]{2,0,1:T(8,128)(2,1)} copy(bf16[8,180,128]{2,0,1:T(8,128)(2,1)} %bitcast.4) | data formatting | bytes 737280
